TPU v7x, 32 devices: a whole 2x2x4 slice. The times are simulated.
32 devices in a mesh: tm: 16 (over z, y, x), head: 2 (over core).
Axes of the slice: x: 2, y: 2, z: 4, core: 2. Of those that a mesh axis runs over, the one named last changes fastest.
Arguments:
- queries: bfloat16 [4096, 3072], P('tm', 'head'), may hold values from -6 to 6
- keys: bfloat16 [2048, 3072], P('tm', 'head'), may hold values from -6 to 6
- values: bfloat16 [2048, 3072], P('tm', 'head'), may hold values from -6 to 6
- out_weight: bfloat16 [3072, 3072], P('head'), may hold values from -0.109375 to 0.109375
- out_grad: bfloat16 [4096, 3072], P('tm', 'head'), may hold values from -6 to 6
- align_lists: int32 [16, 4], replicated, may hold values from -1 to 15, as said below
- block_masks: int32 [32, 3], P('tm'), may hold values from -1 to 3, as said below
Outputs:
- mixed: bfloat16 [4096, 3072], P('tm', 'head')
- query_grad: bfloat16 [4096, 3072], P('tm', 'head')
- key_grad: bfloat16 [2048, 3072], P('tm', 'head')
- value_grad: bfloat16 [2048, 3072], P('tm', 'head')
Inputs may be any that keep to these rules, and one draw needn't show every extreme that they name: `align_lists`: row t holds a band of consecutive audio tile indices in its first slots and -1 in the rest; every listed tile a satisfies (t - 3) <= a < (t + 4). Some slab uses all 4 slots starting at (t - 3), and some slab's band ends at (t + 4) - 1. `block_masks`: row i names one or more consecutive used slots of the list of slab i // 2 in its first entries and -1 in the rest; some row has all 3 entries live.
All inputs are finite; a program needn't handle non-finite values.
Results may differ from a plain program's by a relative error of at most 0.025.
Values may be sent and summed in bfloat16 or wider, within the bound.
A program may use at most 128 MiB of HBM per device.

v0:
```python
import functools
import math

import jax
import jax.numpy as jnp
from jax import lax
from jax.experimental import pallas as pl
from jax.experimental.pallas import tpu as pltpu
from jax.sharding import PartitionSpec as P

HD = 128
TILE = 128
GROUP = 4
LIST = 4
BLOCKS = 3
MESH = pl.DeviceIdType.MESH
NT = (((1,), (1,)), ((), ()))
TN = (((0,), (0,)), ((), ()))
LEAD = 4
AT_S2, AT_S3, AT_CMP, AT_RZ, AT_R1, AT_FIN = 1, 2, 3, 4, 5, 6
F32 = jnp.float32
LOG2E = math.log2(math.e)
BF16 = jnp.bfloat16


def kernel(
    n_tm, n_head, heads, rows,
    align, masks, q_hbm, k_hbm, v_hbm, w_hbm, og_hbm,
    mixed_ref, qg_ref, kg_ref, vg_ref,
    q, w, og, ga_all, att, bias,
    kv, zprev, znext, s3buf,
    own, r3send, r3recv, to_prev, to_next, of_next, of_prev, r1send, r1recv,
    msend, mrecv, mown,
    loc_sem, kv_sem, og_send, og_recv, m_send, m_recv,
    s1_send, s1_recv, z_send, z_recv, s3_send, s3_recv,
    r3_ssem, r3_rsem, zb_send, zb_recv, r1_ssem, r1_rsem,
):
    scale = 1.0 / math.sqrt(HD)
    me = lax.axis_index("tm")
    hd = lax.axis_index("head")
    cols = heads * HD
    planes = n_tm // GROUP
    plane = me // GROUP
    p = me % GROUP
    dx = 1 - 2 * (p % 2)
    dy = 2 - 4 * (p // 2)
    has_prev = plane > 0
    has_next = plane < planes - 1

    unit = 2 if heads % 2 == 0 else 1
    steps = heads // unit

    def sides(c):
        t = c % 2
        d1 = dx * (1 - t) + dy * t
        d2 = dy * (1 - t) + dx * t
        return d1, d2

    def flags(dest, r):
        prev = jnp.int32(0)
        nxt = jnp.int32(0)
        for s in range(LIST):
            a = align[s, dest]
            hit = jnp.logical_and(a >= 0, lax.rem(a + GROUP, GROUP) == r)
            pa = lax.div(a + GROUP, GROUP) - 1
            prev = jnp.where(jnp.logical_and(hit, pa < plane), 1, prev)
            nxt = jnp.where(jnp.logical_and(hit, pa > plane), 1, nxt)
        return prev, nxt

    def rcopy(src, dst, ss, rs, dev):
        return pltpu.make_async_remote_copy(
            src_ref=src, dst_ref=dst, send_sem=ss, recv_sem=rs,
            device_id=dev, device_id_type=MESH,
        )

    def s1_copy(c):
        d1, _ = sides(c)
        return rcopy(kv.at[c, 0], kv.at[c, 1], s1_send.at[c], s1_recv.at[c], {"tm": me + d1})

    def s3_copy(c):
        _, d2 = sides(c)
        return rcopy(
            s3buf.at[c], kv.at[c, pl.ds(2, 2)], s3_send.at[c], s3_recv.at[c], {"tm": me + d2}
        )

    def r3_copy(c):
        _, d2 = sides(c)
        return rcopy(r3send.at[c], r3recv.at[c], r3_ssem.at[c], r3_rsem.at[c], {"tm": me + d2})

    def r1_copy(c):
        d1, _ = sides(c)
        return rcopy(r1send.at[c], r1recv.at[c], r1_ssem.at[c], r1_rsem.at[c], {"tm": me + d1})

    def z_copies(c):
        d1, d2 = sides(c)
        out = []
        for j in range(2):
            r = p + (d1 if j else 0)
            up = jnp.logical_or(r > p, r > p + d2)
            down = jnp.logical_or(r < p, r < p + d2)
            out.append((
                jnp.logical_and(up, has_next),
                rcopy(kv.at[c, j], zprev.at[c, j], z_send.at[c, j], z_recv.at[c, j],
                      {"tm": me + GROUP}),
                jnp.logical_and(up, has_prev),
            ))
            out.append((
                jnp.logical_and(down, has_prev),
                rcopy(kv.at[c, j], znext.at[c, j], z_send.at[c, 2 + j], z_recv.at[c, 2 + j],
                      {"tm": me - GROUP}),
                jnp.logical_and(down, has_next),
            ))
        return out

    def zb_copies(c):
        d1, d2 = sides(c)
        out = []
        for j in range(2):
            r = p + (d1 if j else 0)
            up = jnp.logical_or(r > p, r > p + d2)
            down = jnp.logical_or(r < p, r < p + d2)
            out.append((
                jnp.logical_and(up, has_prev),
                rcopy(to_prev.at[c, j], of_next.at[c, j], zb_send.at[c, j], zb_recv.at[c, j],
                      {"tm": me - GROUP}),
                jnp.logical_and(up, has_next),
            ))
            out.append((
                jnp.logical_and(down, has_next),
                rcopy(to_next.at[c, j], of_prev.at[c, j], zb_send.at[c, 2 + j],
                      zb_recv.at[c, 2 + j], {"tm": me + GROUP}),
                jnp.logical_and(down, has_prev),
            ))
        return out

    def kv_copies(c):
        at = pl.ds(pl.multiple_of(c * HD, HD), HD)
        return (
            pltpu.make_async_copy(k_hbm.at[:, at], kv.at[c, 0, 0], kv_sem.at[c, 0]),
            pltpu.make_async_copy(v_hbm.at[:, at], kv.at[c, 0, 1], kv_sem.at[c, 1]),
        )

    def start_kv(c, carry):
        for copy in kv_copies(c):
            copy.start()
        return carry

    lax.fori_loop(0, heads, start_kv, 0)

    og_own = pl.ds(pl.multiple_of(hd * cols, HD), cols)
    local = (
        pltpu.make_async_copy(og_hbm, og.at[:, og_own], loc_sem.at[0]),
        pltpu.make_async_copy(q_hbm, q, loc_sem.at[1]),
        pltpu.make_async_copy(w_hbm, w, loc_sem.at[2]),
    )
    for copy in local:
        copy.start()

    barrier = pltpu.get_barrier_semaphore()
    pl.semaphore_signal(barrier, inc=1, device_id={"tm": me + dx}, device_id_type=MESH)
    pl.semaphore_signal(barrier, inc=1, device_id={"tm": me + dy}, device_id_type=MESH)

    @pl.when(has_prev)
    def _():
        pl.semaphore_signal(barrier, inc=1, device_id={"tm": me - GROUP}, device_id_type=MESH)

    @pl.when(has_next)
    def _():
        pl.semaphore_signal(barrier, inc=1, device_id={"tm": me + GROUP}, device_id_type=MESH)

    for k in range(1, n_head):
        pl.semaphore_signal(
            barrier, inc=1, device_id={"head": (hd + k) % n_head}, device_id_type=MESH
        )

    near = 2 + (n_head - 1) + jnp.where(has_prev, 1, 0) + jnp.where(has_next, 1, 0)
    pl.semaphore_wait(barrier, near)

    def set_bias():
        row = lax.broadcasted_iota(jnp.int32, (rows, GROUP * TILE), 0)
        col = lax.broadcasted_iota(jnp.int32, (rows, GROUP * TILE), 1)
        for t in range(2):
            d1, d2 = sides(t)
            residues = (p, p + d1, p + d2, p + d1 + d2)
            total = jnp.full((rows, GROUP * TILE), -1e30, F32)
            for i in range(rows // TILE):
                for j, r in enumerate(residues):
                    live = jnp.float32(-1e30)
                    for b in range(BLOCKS):
                        m = masks[i, b]
                        for s in range(LIST):
                            a = align[s, me]
                            hit = jnp.logical_and(m == s, lax.rem(a + GROUP, GROUP) == r)
                            live = jnp.where(hit, jnp.float32(0.0), live)
                    here = jnp.logical_and(row // TILE == i, col // TILE == j)
                    total = jnp.where(here, live, total)
            bias[t] = total

    def og_copy(k):
        return rcopy(
            og_hbm, og.at[:, og_own], og_send.at[k - 1], og_recv.at[k - 1],
            {"head": (hd + k) % n_head},
        )

    def og_arrival(k):
        src = (hd - k + n_head) % n_head
        return rcopy(
            og_hbm, og.at[:, pl.ds(pl.multiple_of(src * cols, HD), cols)],
            og_send.at[k - 1], og_recv.at[k - 1], {"head": (hd + k) % n_head},
        )

    def pick(c, j, prev, nxt):
        return jnp.where(prev > 0, zprev[c, j], jnp.where(nxt > 0, znext[c, j], kv[c, j]))

    def step(k, carry):
        def stage(skew, body):
            n = k - skew
            pl.when(jnp.logical_and(n >= 0, n < steps))(lambda: body([n * unit + u for u in range(unit)]))

        def s1(cs):
            for c in cs:
                for copy in kv_copies(c):
                    copy.wait()
                s1_copy(c).start()

        def s2(cs):
            for c in cs:
                s1_copy(c).wait_recv()
                mine, theirs = z_copies(c)[:2], z_copies(c)[2:]
                for out, copy, _ in mine:
                    pl.when(jnp.logical_and(out, k > AT_S2))(copy.start)
                for out, copy, _ in theirs:
                    pl.when(out)(copy.start)

        def s3(cs):
            for c in cs:
                for _, copy, come in z_copies(c):
                    pl.when(come)(copy.wait_recv)
                d1, d2 = sides(c)
                for j in range(2):
                    prev, nxt = flags(me + d2, p + (d1 if j else 0))
                    s3buf[c, j] = pick(c, j, prev, nxt)
                s3_copy(c).start()

        def cmp(cs):
            for c in cs:
                s3_copy(c).wait_recv()
            at = [pl.ds(pl.multiple_of(c * HD, HD), HD) for c in cs]
            chosen = []
            for c in cs:
                prev, nxt = flags(me, p + sides(c)[0])
                chosen.append(pick(c, 1, prev, nxt))
            each = range(len(cs))
            kh = [
                jnp.concatenate([kv[cs[u], 0, 0], chosen[u][0], kv[cs[u], 2, 0], kv[cs[u], 3, 0]], 0)
                for u in each
            ]
            vh = [
                jnp.concatenate([kv[cs[u], 0, 1], chosen[u][1], kv[cs[u], 2, 1], kv[cs[u], 3, 1]], 0)
                for u in each
            ]
            qh = [q[:, at[u]] for u in each]
            ga = [ga_all[:, at[u]] for u in each]
            scores = [lax.dot_general(qh[u], kh[u], NT, preferred_element_type=F32) for u in each]
            gp = [lax.dot_general(ga[u], vh[u], NT, preferred_element_type=F32) for u in each]
            scores = [scores[u] * (scale * LOG2E) + bias[cs[u] % 2] for u in each]
            e = [jnp.exp2(x - jnp.max(x, -1, keepdims=True)) for x in scores]
            probs = [x * (1.0 / jnp.sum(x, -1, keepdims=True)) for x in e]
            weights = [x.astype(BF16) for x in probs]
            attended = [
                jnp.dot(weights[u], vh[u], preferred_element_type=F32).astype(BF16) for u in each
            ]
            vt = [lax.dot_general(weights[u], ga[u], TN, preferred_element_type=F32) for u in each]
            delta = [
                jnp.sum(ga[u].astype(F32) * attended[u].astype(F32), -1, keepdims=True) for u in each
            ]
            gs = [(probs[u] * (gp[u] - delta[u])).astype(BF16) for u in each]
            kt = [
                lax.dot_general(gs[u], qh[u], TN, preferred_element_type=F32) * scale for u in each
            ]
            for u in each:
                for j in range(2):
                    r3send[cs[u], j, 0] = kt[u][(2 + j) * TILE:(3 + j) * TILE].astype(BF16)
                    r3send[cs[u], j, 1] = vt[u][(2 + j) * TILE:(3 + j) * TILE].astype(BF16)
            for c in cs:
                r3_copy(c).start()
            for u in each:
                qg = jnp.dot(gs[u], kh[u], preferred_element_type=F32) * scale
                qg_ref[:, at[u]] = qg.astype(BF16)
                att[:, at[u]] = attended[u]
                for j in range(2):
                    own[cs[u], j, 0] = kt[u][j * TILE:(j + 1) * TILE]
                    own[cs[u], j, 1] = vt[u][j * TILE:(j + 1) * TILE]

        def rz(cs):
            for c in cs:
                d1, d2 = sides(c)
                r3_copy(c).wait_recv()
                for j in range(2):
                    r = p + (d1 if j else 0)
                    mp, mn = flags(me, r)
                    op, on = flags(me + d2, r)
                    mp, mn, op, on = (x.astype(F32) for x in (mp, mn, op, on))
                    mine = own[c, j]
                    other = r3recv[c, j].astype(F32)
                    to_prev[c, j] = (mine * mp + other * op).astype(BF16)
                    to_next[c, j] = (mine * mn + other * on).astype(BF16)
                    own[c, j] = mine * (1.0 - mp - mn) + other * (1.0 - op - on)
                for out, copy, _ in zb_copies(c)[2:]:
                    pl.when(out)(copy.start)
            for c in cs:
                for out, copy, _ in zb_copies(c)[:2]:
                    pl.when(out)(copy.start)

        def back(c, j):
            copies = zb_copies(c)[2 * j:2 * j + 2]
            for _, copy, come in copies:
                pl.when(come)(copy.wait_recv)
            total = own[c, j]
            total = total + jnp.where(copies[0][2], of_next[c, j].astype(F32), 0.0)
            return total + jnp.where(copies[1][2], of_prev[c, j].astype(F32), 0.0)

        def r1(cs):
            for c in cs:
                r1send[c] = back(c, 1).astype(BF16)
                r1_copy(c).start()

        def fin(cs):
            for c in cs:
                total = back(c, 0)
                r1_copy(c).wait_recv()
                at = pl.ds(pl.multiple_of(c * HD, HD), HD)
                kg_ref[:, at] = (total[0] + r1recv[c, 0].astype(F32)).astype(BF16)
                vg_ref[:, at] = (total[1] + r1recv[c, 1].astype(F32)).astype(BF16)

        @pl.when(k == 0)
        def _():
            for kk in range(1, n_head):
                og_copy(kk).start()
            for n in range(lead):
                s1([n * unit + u for u in range(unit)])
                if n == 0:
                    for u in range(unit):
                        for out, copy, _ in z_copies(u)[:2]:
                            pl.when(out)(copy.start)
            set_bias()

        stage(-lead, s1)
        stage(AT_S2, s2)

        @pl.when(k == AT_S2)
        def _():
            for copy in local:
                copy.wait()
            for kk in range(1, n_head):
                og_arrival(kk).wait_recv()
            grads(0, blocks // 2)

        stage(AT_S3, s3)

        @pl.when(k == AT_S3)
        def _():
            grads(blocks // 2, blocks)

        stage(AT_CMP, cmp)

        @pl.when(k == steps + AT_CMP)
        def _():
            for kk in range(1, n_head):
                mix(kk)

        stage(AT_RZ, rz)
        stage(AT_R1, r1)

        @pl.when(k == steps + AT_CMP)
        def _():
            mix(0)

        @pl.when(k == steps + AT_FIN - 1)
        def _():
            for kk in range(1, n_head):
                m_copy(kk).wait_recv()
            total = mown[...].astype(F32)
            for kk in range(1, n_head):
                total = total + mrecv[kk - 1].astype(F32)
            mixed_ref[...] = total.astype(BF16)

        stage(AT_FIN, fin)
        return carry

    lead = min(LEAD, steps)
    block = 256 if cols % 256 == 0 else 128
    blocks = cols // block
    def grads(first, last):
        def one(n, carry):
            at = pl.ds(pl.multiple_of(n * block, 128), block)
            ga = lax.dot_general(og[...], w[at, :], NT, preferred_element_type=F32)
            ga_all[:, at] = ga.astype(BF16)
            return carry

        lax.fori_loop(first, last, one, 0)

    def m_copy(k):
        return rcopy(
            msend.at[k - 1], mrecv.at[k - 1], m_send.at[k - 1], m_recv.at[k - 1],
            {"head": (hd + k) % n_head},
        )

    def mix(k):
        base = ((hd + k) % n_head) * cols
        out = msend.at[k - 1] if k else mown

        def one(n, carry):
            src = pl.ds(pl.multiple_of(base + n * block, 128), block)
            dst = pl.ds(pl.multiple_of(n * block, 128), block)
            part = jnp.dot(att[...], w[:, src], preferred_element_type=F32)
            out[:, dst] = part.astype(BF16)
            return carry

        lax.fori_loop(0, blocks, one, 0)
        if k:
            m_copy(k).start()

    lax.fori_loop(0, steps + AT_FIN, step, 0)

    def drain(c, carry):
        s1_copy(c).wait_send()
        s3_copy(c).wait_send()
        r3_copy(c).wait_send()
        r1_copy(c).wait_send()
        for out, copy, _ in z_copies(c) + zb_copies(c):
            pl.when(out)(copy.wait_send)
        return carry

    lax.fori_loop(0, heads, drain, 0)
    for k in range(1, n_head):
        og_copy(k).wait_send()
        m_copy(k).wait_send()


def hand_on(*refs):
    sems = refs[-1]
    n = len(refs) // 2
    copies = [pltpu.make_async_copy(refs[i], refs[n + i], sems.at[i]) for i in range(n)]
    for copy in copies:
        copy.start()
    for copy in copies:
        copy.wait()


def local(n_tm, n_head, queries, keys, values, out_weight, out_grad, align_lists, block_masks):
    rows, cols = queries.shape
    heads = cols // HD
    width = out_weight.shape[1]
    others = max(n_head - 1, 1)
    pair = (2, TILE, HD)
    hbm = pl.BlockSpec(memory_space=pltpu.HBM)
    vmem = pl.BlockSpec(memory_space=pltpu.VMEM)
    smem = pl.BlockSpec(memory_space=pltpu.SMEM)
    dma = pltpu.SemaphoreType.DMA
    V = pltpu.VMEM
    shapes = (
        jax.ShapeDtypeStruct((rows, cols), BF16),
        jax.ShapeDtypeStruct((rows, cols), BF16),
        jax.ShapeDtypeStruct(keys.shape, BF16),
        jax.ShapeDtypeStruct(keys.shape, BF16),
    )
    results = pl.pallas_call(
        functools.partial(kernel, n_tm, n_head, heads, rows),
        out_shape=tuple(V(x.shape, BF16) for x in shapes),
        in_specs=[smem, smem, hbm, hbm, hbm, hbm, hbm],
        out_specs=(vmem,) * 4,
        scratch_shapes=[
            V((rows, cols), BF16),
            V((cols, width), BF16),
            V((rows, width), BF16),
            V((rows, cols), BF16),
            V((rows, cols), BF16),
            V((2, rows, GROUP * TILE), F32),
            V((heads, 4) + pair, BF16),
            V((heads, 2) + pair, BF16),
            V((heads, 2) + pair, BF16),
            V((heads, 2) + pair, BF16),
            V((heads, 2) + pair, F32),
            V((heads, 2) + pair, BF16),
            V((heads, 2) + pair, BF16),
            V((heads, 2) + pair, BF16),
            V((heads, 2) + pair, BF16),
            V((heads, 2) + pair, BF16),
            V((heads, 2) + pair, BF16),
            V((heads,) + pair, BF16),
            V((heads,) + pair, BF16),
            V((others, rows, cols), BF16),
            V((others, rows, cols), BF16),
            V((rows, cols), BF16),
            dma((3,)),
            dma((heads, 2)),
            dma((others,)),
            dma((others,)),
            dma((others,)),
            dma((others,)),
            dma((heads,)),
            dma((heads,)),
            dma((heads, 4)),
            dma((heads, 4)),
            dma((heads,)),
            dma((heads,)),
            dma((heads,)),
            dma((heads,)),
            dma((heads, 4)),
            dma((heads, 4)),
            dma((heads,)),
            dma((heads,)),
        ],
        compiler_params=pltpu.CompilerParams(
            collective_id=0, has_side_effects=True, vmem_limit_bytes=59 * 1024 * 1024
        ),
        cost_estimate=pl.CostEstimate(
            flops=4 * rows * cols * width + 12 * rows * GROUP * TILE * cols,
            bytes_accessed=2 * cols * width, transcendentals=rows * GROUP * TILE * heads,
        ),
    )(align_lists.T, block_masks, queries, keys, values, out_weight, out_grad)
    return pl.pallas_call(
        hand_on,
        out_shape=shapes,
        in_specs=[vmem] * 4,
        out_specs=(pl.BlockSpec(memory_space=pltpu.HBM),) * 4,
        scratch_shapes=[dma((4,))],
    )(*results)


def solution(mesh):
    split = P("tm", "head")
    return jax.shard_map(
        functools.partial(local, mesh.shape["tm"], mesh.shape["head"]),
        mesh=mesh,
        in_specs=(split, split, split, P("head", None), split, P(), P("tm", None)),
        out_specs=(split, split, split, split),
        check_vma=False,
    )
```

profile of v0, /device:TPU:0, one launch (start us, length us, event | category | flops | bytes accessed | tf_op | source)
XLA Modules:
  0.0 72.3 jit_solution(420609209317049288)
XLA Ops:
  0.6 65.3 %shard_map.102 = (bf16[256,1536]{1,0:T(8,128)(2,1)S(1)}, bf16[256,1536]{1,0:T(8,128)(2,1)S(1)}, bf16[128,1536]{1,0:T(8,128)(2,1)S(1)}, bf16[128,1536]{1,0:T(8,128)(2,1)S(1)}) custom-call(s32[4,16]{1,0:T(4,128)} %bitcast.1, s32[2,3]{1,0:T(2,128)} %masks.1, bf16[256,1536]{1,0:T(8,128)(2,1)} %q_hbm.1, bf16[128,1536]{1,0:T(8,128)(2,1)} %k_hbm.1, ...), custom_call_target="tpu_custom_call" | custom-call | flops 7247757312 | bytes 9437184 | tf_op jit(solution)/shard_map/pallas_call | solution.py:468
  65.9 0.0 copy-start
  66.0 0.9 %copy-done = bf16[256,1536]{1,0:T(8,128)(2,1)} copy-done((bf16[256,1536]{1,0:T(8,128)(2,1)}, bf16[256,1536]{1,0:T(8,128)(2,1)S(1)}, u32[]{:S(2)}) %copy-start) | copy-done | bytes 786456
  66.8 0.0 copy-start.1
  66.8 0.9 %copy-done.1 = bf16[256,1536]{1,0:T(8,128)(2,1)} copy-done((bf16[256,1536]{1,0:T(8,128)(2,1)}, bf16[256,1536]{1,0:T(8,128)(2,1)S(1)}, u32[]{:S(2)}) %copy-start.1) | copy-done | bytes 786456
  67.7 0.0 copy-start.2
  67.7 0.7 %copy-done.2 = bf16[128,1536]{1,0:T(8,128)(2,1)} copy-done((bf16[128,1536]{1,0:T(8,128)(2,1)}, bf16[128,1536]{1,0:T(8,128)(2,1)S(1)}, u32[]{:S(2)}) %copy-start.2) | copy-done | bytes 393240
  68.5 0.0 copy-start.3
  68.5 0.8 %copy-done.3 = bf16[128,1536]{1,0:T(8,128)(2,1)} copy-done((bf16[128,1536]{1,0:T(8,128)(2,1)}, bf16[128,1536]{1,0:T(8,128)(2,1)S(1)}, u32[]{:S(2)}) %copy-start.3) | copy-done | bytes 393240
  69.3 3.0 %shard_map.103 = (bf16[256,1536]{1,0:T(8,128)(2,1)}, bf16[256,1536]{1,0:T(8,128)(2,1)}, bf16[128,1536]{1,0:T(8,128)(2,1)}, bf16[128,1536]{1,0:T(8,128)(2,1)}) custom-call(bf16[256,1536]{1,0:T(8,128)(2,1)} %copy-done, bf16[256,1536]{1,0:T(8,128)(2,1)} %copy-done.1, bf16[128,1536]{1,0:T(8,128)(2,1)} %copy-done.2, bf16[128,1536]{1,0:T(8,128)(2,1)} %copy-done.3), custom_call_target="tpu_custom_call" | custom-call | tf_op jit(solution)/shard_map/pallas_call | solution.py:523
Async XLA Ops:
  65.9 0.9 %copy-start = (bf16[256,1536]{1,0:T(8,128)(2,1)}, bf16[256,1536]{1,0:T(8,128)(2,1)S(1)}, u32[]{:S(2)}) copy-start(bf16[256,1536]{1,0:T(8,128)(2,1)S(1)} %get-tuple-element.8.refs_0_) | copy-start | bytes 2359300
  66.8 0.9 %copy-start.1 = (bf16[256,1536]{1,0:T(8,128)(2,1)}, bf16[256,1536]{1,0:T(8,128)(2,1)S(1)}, u32[]{:S(2)}) copy-start(bf16[256,1536]{1,0:T(8,128)(2,1)S(1)} %get-tuple-element.9.refs_1_) | copy-start | bytes 2359300
  67.7 0.7 %copy-start.2 = (bf16[128,1536]{1,0:T(8,128)(2,1)}, bf16[128,1536]{1,0:T(8,128)(2,1)S(1)}, u32[]{:S(2)}) copy-start(bf16[128,1536]{1,0:T(8,128)(2,1)S(1)} %get-tuple-element.10.refs_2_) | copy-start | bytes 1179652
  68.5 0.8 %copy-start.3 = (bf16[128,1536]{1,0:T(8,128)(2,1)}, bf16[128,1536]{1,0:T(8,128)(2,1)S(1)}, u32[]{:S(2)}) copy-start(bf16[128,1536]{1,0:T(8,128)(2,1)S(1)} %get-tuple-element.11.refs_3_) | copy-start | bytes 1179652
where the time goes:
time: 72.5 us; the launch traced here: 72.3 us
  Pallas kernels  68.3 us (94%)
  local copies, waits for them, and re-layouts  3.31 us (5%)
    pallas_call x1, Pallas kernels, local(): pl.pallas_call(functools.partial(kernel, n_tm, n_head, heads, rows), out_...  65.3 us
    unnamed x8, local copies, waits for them, and re-layouts  3.31 us
    pallas_call x1, Pallas kernels, local(): pl.pallas_call(hand_on, out_shape=shapes, in_specs=[vmem] * 4, out_specs=...  3.01 us

commit v1 on v0

--- a/solution.py
+++ b/solution.py
@@ -17,7 +17,7 @@
 NT = (((1,), (1,)), ((), ()))
 TN = (((0,), (0,)), ((), ()))
 LEAD = 4
-AT_S2, AT_S3, AT_CMP, AT_RZ, AT_R1, AT_FIN = 1, 2, 3, 4, 5, 6
+AT_S2, AT_S3, AT_CMP, AT_RZ = 1, 2, 3, 4
 F32 = jnp.float32
 LOG2E = math.log2(math.e)
 BF16 = jnp.bfloat16
@@ -212,10 +212,41 @@
     def pick(c, j, prev, nxt):
         return jnp.where(prev > 0, zprev[c, j], jnp.where(nxt > 0, znext[c, j], kv[c, j]))
 
+    def back(c, j):
+        copies = zb_copies(c)[2 * j:2 * j + 2]
+        for _, copy, come in copies:
+            pl.when(come)(copy.wait_recv)
+        total = own[c, j]
+        total = total + jnp.where(copies[0][2], of_next[c, j].astype(F32), 0.0)
+        return total + jnp.where(copies[1][2], of_prev[c, j].astype(F32), 0.0)
+
+    def r1(cs):
+        for c in cs:
+            r1send[c] = back(c, 1).astype(BF16)
+            r1_copy(c).start()
+
+    def fin(cs):
+        for c in cs:
+            total = back(c, 0)
+            r1_copy(c).wait_recv()
+            at = pl.ds(pl.multiple_of(c * HD, HD), HD)
+            kg_ref[:, at] = (total[0] + r1recv[c, 0].astype(F32)).astype(BF16)
+            vg_ref[:, at] = (total[1] + r1recv[c, 1].astype(F32)).astype(BF16)
+
+    def pair(n):
+        return [n * unit + u for u in range(unit)]
+
+    def each_pair(first, last, body):
+        def one(n, carry):
+            body(pair(n))
+            return carry
+
+        lax.fori_loop(first, last, one, 0)
+
     def step(k, carry):
         def stage(skew, body):
             n = k - skew
-            pl.when(jnp.logical_and(n >= 0, n < steps))(lambda: body([n * unit + u for u in range(unit)]))
+            pl.when(jnp.logical_and(n >= 0, n < steps))(lambda: body(pair(n)))
 
         def s1(cs):
             for c in cs:
@@ -312,33 +343,12 @@
                 for out, copy, _ in zb_copies(c)[:2]:
                     pl.when(out)(copy.start)
 
-        def back(c, j):
-            copies = zb_copies(c)[2 * j:2 * j + 2]
-            for _, copy, come in copies:
-                pl.when(come)(copy.wait_recv)
-            total = own[c, j]
-            total = total + jnp.where(copies[0][2], of_next[c, j].astype(F32), 0.0)
-            return total + jnp.where(copies[1][2], of_prev[c, j].astype(F32), 0.0)
-
-        def r1(cs):
-            for c in cs:
-                r1send[c] = back(c, 1).astype(BF16)
-                r1_copy(c).start()
-
-        def fin(cs):
-            for c in cs:
-                total = back(c, 0)
-                r1_copy(c).wait_recv()
-                at = pl.ds(pl.multiple_of(c * HD, HD), HD)
-                kg_ref[:, at] = (total[0] + r1recv[c, 0].astype(F32)).astype(BF16)
-                vg_ref[:, at] = (total[1] + r1recv[c, 1].astype(F32)).astype(BF16)
-
         @pl.when(k == 0)
         def _():
             for kk in range(1, n_head):
                 og_copy(kk).start()
             for n in range(lead):
-                s1([n * unit + u for u in range(unit)])
+                s1(pair(n))
                 if n == 0:
                     for u in range(unit):
                         for out, copy, _ in z_copies(u)[:2]:
@@ -368,24 +378,9 @@
         def _():
             for kk in range(1, n_head):
                 mix(kk)
+            each_pair(0, steps - 2, r1)
 
         stage(AT_RZ, rz)
-        stage(AT_R1, r1)
-
-        @pl.when(k == steps + AT_CMP)
-        def _():
-            mix(0)
-
-        @pl.when(k == steps + AT_FIN - 1)
-        def _():
-            for kk in range(1, n_head):
-                m_copy(kk).wait_recv()
-            total = mown[...].astype(F32)
-            for kk in range(1, n_head):
-                total = total + mrecv[kk - 1].astype(F32)
-            mixed_ref[...] = total.astype(BF16)
-
-        stage(AT_FIN, fin)
         return carry
 
     lead = min(LEAD, steps)
@@ -421,7 +416,17 @@
         if k:
             m_copy(k).start()
 
-    lax.fori_loop(0, steps + AT_FIN, step, 0)
+    lax.fori_loop(0, steps + AT_RZ, step, 0)
+    r1(pair(steps - 2))
+    mix(0)
+    r1(pair(steps - 1))
+    for kk in range(1, n_head):
+        m_copy(kk).wait_recv()
+    total = mown[...].astype(F32)
+    for kk in range(1, n_head):
+        total = total + mrecv[kk - 1].astype(F32)
+    mixed_ref[...] = total.astype(BF16)
+    each_pair(0, steps, fin)
 
     def drain(c, carry):
         s1_copy(c).wait_send()
@@ -526,6 +531,7 @@
         in_specs=[vmem] * 4,
         out_specs=(pl.BlockSpec(memory_space=pltpu.HBM),) * 4,
         scratch_shapes=[dma((4,))],
+        compiler_params=pltpu.CompilerParams(vmem_limit_bytes=1024 * 1024),
     )(*results)
 
 

time: 72.5 us -> 65 us (0.90)
  Pallas kernels: 68.3 us -> 64.2 us
  local copies, waits for them, and re-layouts: 3.31 us -> 0 us
    unnamed x8 -> x0, local copies, waits for them, and re-layouts: 3.31 us -> none
    pallas_call x1, Pallas kernels: 65.3 us -> 62.7 us  [local(): pl.pallas_call(functools.partial(kernel, n_tm, n_head, heads, rows), out_...]
    pallas_call x1, Pallas kernels: 3.01 us -> 1.43 us  [local(): pl.pallas_call(hand_on, out_shape=shapes, in_specs=[vmem] * 4, out_specs=...]
where the time goes in v1:
time: 65 us; the launch traced here: 64.8 us
  Pallas kernels  64.2 us (99%)
    pallas_call x1, Pallas kernels, local(): pl.pallas_call(functools.partial(kernel, n_tm, n_head, heads, rows), out_...  62.7 us
    pallas_call x1, Pallas kernels, local(): pl.pallas_call(hand_on, out_shape=shapes, in_specs=[vmem] * 4, out_specs=...  1.43 us

profile of v1, /device:TPU:0, one launch (start us, length us, event | category | flops | bytes accessed | tf_op | source)
XLA Modules:
  0.0 64.8 jit_solution(490733170837219924)
XLA Ops:
  0.6 62.7 %shard_map.102 = (bf16[256,1536]{1,0:T(8,128)(2,1)S(1)}, bf16[256,1536]{1,0:T(8,128)(2,1)S(1)}, bf16[128,1536]{1,0:T(8,128)(2,1)S(1)}, bf16[128,1536]{1,0:T(8,128)(2,1)S(1)}) custom-call(s32[4,16]{1,0:T(4,128)} %bitcast.1, s32[2,3]{1,0:T(2,128)} %masks.1, bf16[256,1536]{1,0:T(8,128)(2,1)} %q_hbm.1, bf16[128,1536]{1,0:T(8,128)(2,1)} %k_hbm.1, ...), custom_call_target="tpu_custom_call" | custom-call | flops 7247757312 | bytes 9437184 | tf_op jit(solution)/shard_map/pallas_call | solution.py:473
  63.4 1.4 %shard_map.103 = (bf16[256,1536]{1,0:T(8,128)(2,1)}, bf16[256,1536]{1,0:T(8,128)(2,1)}, bf16[128,1536]{1,0:T(8,128)(2,1)}, bf16[128,1536]{1,0:T(8,128)(2,1)}) custom-call(bf16[256,1536]{1,0:T(8,128)(2,1)S(1)} %get-tuple-element.8.refs_0_, bf16[256,1536]{1,0:T(8,128)(2,1)S(1)} %get-tuple-element.9.refs_1_, bf16[128,1536]{1,0:T(8,128)(2,1)S(1)} %get-tuple-element.10.refs_2_, ...), custom_call_target="tpu_custom_call" | custom-call | tf_op jit(solution)/shard_map/pallas_call | solution.py:528

commit v2 on v1

--- a/solution.py
+++ b/solution.py
@@ -16,7 +16,7 @@
 MESH = pl.DeviceIdType.MESH
 NT = (((1,), (1,)), ((), ()))
 TN = (((0,), (0,)), ((), ()))
-LEAD = 4
+LEAD = 5
 AT_S2, AT_S3, AT_CMP, AT_RZ = 1, 2, 3, 4
 F32 = jnp.float32
 LOG2E = math.log2(math.e)
@@ -325,23 +325,32 @@
 
         def rz(cs):
             for c in cs:
-                d1, d2 = sides(c)
                 r3_copy(c).wait_recv()
-                for j in range(2):
-                    r = p + (d1 if j else 0)
-                    mp, mn = flags(me, r)
-                    op, on = flags(me + d2, r)
-                    mp, mn, op, on = (x.astype(F32) for x in (mp, mn, op, on))
-                    mine = own[c, j]
-                    other = r3recv[c, j].astype(F32)
-                    to_prev[c, j] = (mine * mp + other * op).astype(BF16)
-                    to_next[c, j] = (mine * mn + other * on).astype(BF16)
-                    own[c, j] = mine * (1.0 - mp - mn) + other * (1.0 - op - on)
-                for out, copy, _ in zb_copies(c)[2:]:
-                    pl.when(out)(copy.start)
-            for c in cs:
-                for out, copy, _ in zb_copies(c)[:2]:
-                    pl.when(out)(copy.start)
+            for j in (1, 0):
+                for c in cs:
+                    split(c, j)
+
+        def split(c, j):
+            d1, d2 = sides(c)
+            r = p + (d1 if j else 0)
+            mp, mn = flags(me, r)
+            op, on = flags(me + d2, r)
+            mp, mn, op, on = (x.astype(F32) for x in (mp, mn, op, on))
+            (prev_out, prev_copy, _), (next_out, next_copy, _) = zb_copies(c)[2 * j:2 * j + 2]
+
+            @pl.when(prev_out)
+            def _():
+                to_prev[c, j] = (own[c, j] * mp + r3recv[c, j].astype(F32) * op).astype(BF16)
+                prev_copy.start()
+
+            @pl.when(next_out)
+            def _():
+                to_next[c, j] = (own[c, j] * mn + r3recv[c, j].astype(F32) * on).astype(BF16)
+                next_copy.start()
+
+            own[c, j] = (
+                own[c, j] * (1.0 - mp - mn) + r3recv[c, j].astype(F32) * (1.0 - op - on)
+            )
 
         @pl.when(k == 0)
         def _():

time: 65 us -> 64.8 us (level)
  no operation moved by 1% of the time
where the time goes in v2:
time: 64.8 us; the launch traced here: 64.6 us
  Pallas kernels  64 us (99%)
    pallas_call x1, Pallas kernels, local(): pl.pallas_call(functools.partial(kernel, n_tm, n_head, heads, rows), out_...  62.5 us
    pallas_call x1, Pallas kernels, local(): pl.pallas_call(hand_on, out_shape=shapes, in_specs=[vmem] * 4, out_specs=...  1.43 us

profile of v2, /device:TPU:0, one launch (start us, length us, event | category | flops | bytes accessed | tf_op | source)
XLA Modules:
  0.0 64.6 jit_solution(5519581275390346761)
XLA Ops:
  0.6 62.5 %shard_map.102 = (bf16[256,1536]{1,0:T(8,128)(2,1)S(1)}, bf16[256,1536]{1,0:T(8,128)(2,1)S(1)}, bf16[128,1536]{1,0:T(8,128)(2,1)S(1)}, bf16[128,1536]{1,0:T(8,128)(2,1)S(1)}) custom-call(s32[4,16]{1,0:T(4,128)} %bitcast.1, s32[2,3]{1,0:T(2,128)} %masks.1, bf16[256,1536]{1,0:T(8,128)(2,1)} %q_hbm.1, bf16[128,1536]{1,0:T(8,128)(2,1)} %k_hbm.1, ...), custom_call_target="tpu_custom_call" | custom-call | flops 7247757312 | bytes 9437184 | tf_op jit(solution)/shard_map/pallas_call | solution.py:482
  63.2 1.4 %shard_map.103 = (bf16[256,1536]{1,0:T(8,128)(2,1)}, bf16[256,1536]{1,0:T(8,128)(2,1)}, bf16[128,1536]{1,0:T(8,128)(2,1)}, bf16[128,1536]{1,0:T(8,128)(2,1)}) custom-call(bf16[256,1536]{1,0:T(8,128)(2,1)S(1)} %get-tuple-element.8.refs_0_, bf16[256,1536]{1,0:T(8,128)(2,1)S(1)} %get-tuple-element.9.refs_1_, bf16[128,1536]{1,0:T(8,128)(2,1)S(1)} %get-tuple-element.10.refs_2_, ...), custom_call_target="tpu_custom_call" | custom-call | tf_op jit(solution)/shard_map/pallas_call | solution.py:537
